TPU v7x, 32 devices: a whole 2x2x4 slice. The times are simulated.
32 devices in a mesh: samp: 16 (over z, y, core), blk: 2 (over x).
Axes of the slice: x: 2, y: 2, z: 4, core: 2. Of those that a mesh axis runs over, the one named last changes fastest.
Arguments:
- genotypes: int32 [65536, 2048], P('samp', 'blk'), may hold values from 0 to 2
- traits: bfloat16 [65536, 64], P('samp'), may hold values from -6 to 6
- penalty_index: int32 [5], replicated, may hold values from 0 to 9
Outputs:
- level_gram: float32 [64, 10, 10], P('blk')
- level_cross: float32 [64, 10], P('blk')
All inputs are finite; a program needn't handle non-finite values.
Results may differ from a plain program's by a relative error of at most 0.0004.
Values may be sent and summed in bfloat16 or wider, within the bound.
No kernel may reach another device: no remote copies, remote signals or barrier semaphores. Data moves between devices by JAX's collectives and lax.ppermute only.
A program may use at most 192 MiB of HBM per device.

v0:
```python
import jax
import jax.numpy as jnp
from jax import lax
from jax.sharding import PartitionSpec as P


def ridge_solve(gstd, rhs, penalty):
    eye = jnp.eye(gstd.shape[0], dtype=jnp.float32)
    factor = jnp.linalg.cholesky(gstd + penalty * eye)
    return jax.scipy.linalg.cho_solve((factor, True), rhs)


def level_sums(parts, trait_rows):
    gram = jnp.einsum("btrn,ctsn->tbrcs", parts, parts, preferred_element_type=jnp.float32)
    cross = jnp.einsum("btrn,nt->tbr", parts, trait_rows, preferred_element_type=jnp.float32)
    count = parts.shape[1]
    stack = parts.shape[0] * parts.shape[2]
    return (gram.reshape(count, stack, stack), cross.reshape(count, stack))


def local(genotypes, traits, penalty_index):
    hi = lax.Precision.HIGHEST
    dosage = genotypes.astype(jnp.bfloat16)
    nvars = dosage.shape[1]
    ntraits = traits.shape[1]
    total = jnp.float32(dosage.shape[0] * lax.axis_size("samp"))
    lam = total * jnp.exp2((penalty_index.astype(jnp.float32) - 8.0) / 2.0)
    gram_part = jnp.einsum("nm,nk->mk", dosage, dosage, preferred_element_type=jnp.float32)
    xty_part = jnp.einsum("nm,nt->mt", dosage, traits, preferred_element_type=jnp.float32)
    col_part = jnp.sum(dosage, axis=0, dtype=jnp.float32)
    ysum_part = jnp.sum(traits, axis=0, dtype=jnp.float32)
    gram, xty, colsum, ysum = lax.psum((gram_part, xty_part, col_part, ysum_part), "samp")
    mean = colsum / total
    spread = jnp.sqrt(jnp.diagonal(gram) / total - mean * mean + 1e-05)
    gstd = (gram - total * mean[:, None] * mean[None, :]) / (spread[:, None] * spread[None, :])
    rhs = (xty - mean[:, None] * ysum[None, :]) / spread[:, None]
    beta = jax.vmap(ridge_solve, in_axes=(None, None, 0))(gstd, rhs, lam)
    coef = (beta / spread[None, :, None]).astype(jnp.bfloat16)
    offset = jnp.einsum("rmt,m->rt", coef.astype(jnp.float32), mean, precision=hi)
    pred = jnp.einsum("rmt,nm->trn", coef, dosage, preferred_element_type=jnp.float32)
    pred = (pred - offset.T[:, :, None]).astype(jnp.bfloat16)
    nblk = lax.axis_size("blk")
    blk_rank = lax.axis_index("blk")
    local_traits = ntraits // nblk
    parts = lax.all_to_all(pred[None], "blk", split_axis=1, concat_axis=0, tiled=True)
    trait_rows = lax.dynamic_slice_in_dim(traits, blk_rank * local_traits, local_traits, 1)
    gram_own, cross_own = level_sums(parts, trait_rows)
    level_gram, level_cross = lax.psum((gram_own, cross_own), "samp")
    return (level_gram / nvars, level_cross / nvars)


def solution(mesh):
    placed = (P("samp", "blk"), P("samp", None), P())
    return jax.shard_map(
        local,
        mesh=mesh,
        in_specs=placed,
        out_specs=(P("blk", None, None), P("blk", None)),
        check_vma=False,
    )
```

profile of v0, /device:TPU:0, one launch (start us, length us, event | category | flops | bytes accessed | tf_op | source)
XLA Modules:
  0.0 1753.2 jit_solution(15345960124817691053)
XLA Ops:
  7.2 7.6 convert_reduce_fusion
  14.9 10.5 fusion.180
  27.9 37.1 %all-reduce.2 = (f32[1024]{0:T(1024)S(1)}, f32[64]{0:T(128)S(1)}) all-reduce(f32[1024]{0:T(1024)S(1)} %get-tuple-element.32, f32[64]{0:T(128)S(1)} %convert_reduce_fusion.1), channel_id=1, replica_groups=mesh['samp'=16,'blk'=2] {'samp'}, use_global_device_ids=true, to_apply=%region_2.0 | all-reduce | flops 1088 | bytes 8704 | tf_op jit(solution)/shard_map/psum | solution.py:32
  66.3 4.4 fusion.23
  70.7 74.7 %all-reduce.6.cloned.1.call-done = (f32[1024,1024]{1,0:T(8,128)}, f32[1024,64]{0,1:T(8,128)}) async-done(((f32[1024,1024]{1,0:T(8,128)}, f32[1024,64]{0,1:T(8,128)}), (f32[1024,1024]{1,0:T(8,128)}, f32[1024,64]{0,1:T(8,128)})) %all-reduce.6.cloned.1.call-update) | async-done | bytes 4456464 | tf_op jit(solution)/shard_map/psum | solution.py:32
  145.4 17.3 gather_fusion
  162.8 5.1 multiply_divide_fusion
  170.6 5.3 copy.145
  175.9 8.8 add_multiply_fusion
  184.8 7.0 copy-done.1
  191.8 58.6 %custom-call.74 = f32[5,128,128]{2,1,0:T(8,128)S(1)} custom-call(f32[5,128,128]{2,1,0:T(8,128)S(1)} %cholesky.578), custom_call_target="Cholesky" | custom-call | tf_op jit(solution)/shard_map/vmap(jit(cholesky))/cholesky | solution.py:9
  250.4 49.3 %custom-call.75 = f32[5,1,128,128]{2,3,1,0:T(8,128)S(1)} custom-call(f32[5,1,128,128]{3,2,1,0:T(8,128)S(1)} %select_bitcast_fusion.6), custom_call_target="InvertDiagBlocksLowerTriangular" | custom-call | tf_op jit(solution)/shard_map/vmap(jit(cholesky))/cholesky | solution.py:9
  299.8 9.6 cholesky.253
  309.4 5.1 constant_dynamic-update-slice_fusion.50
  314.5 3.7 slice_subtract_fusion
  319.0 59.4 %custom-call.76 = f32[5,128,128]{2,1,0:T(8,128)S(1)} custom-call(f32[5,128,128]{2,1,0:T(8,128)} %cholesky.582), custom_call_target="Cholesky" | custom-call | tf_op jit(solution)/shard_map/vmap(jit(cholesky))/cholesky | solution.py:9
  379.4 50.9 %custom-call.77 = f32[5,1,128,128]{2,3,1,0:T(8,128)} custom-call(f32[5,1,128,128]{3,2,1,0:T(8,128)} %get-tuple-element.47), custom_call_target="InvertDiagBlocksLowerTriangular" | custom-call | tf_op jit(solution)/shard_map/vmap(jit(cholesky))/cholesky | solution.py:9
  430.3 4.2 fusion.47
  434.5 6.4 slice_subtract_fusion.1
  441.6 59.4 %custom-call.78 = f32[5,128,128]{2,1,0:T(8,128)S(1)} custom-call(f32[5,128,128]{2,1,0:T(8,128)} %cholesky.587), custom_call_target="Cholesky" | custom-call | tf_op jit(solution)/shard_map/vmap(jit(cholesky))/cholesky | solution.py:9
  502.0 50.7 %custom-call.79 = f32[5,1,128,128]{2,3,1,0:T(8,128)} custom-call(f32[5,1,128,128]{3,2,1,0:T(8,128)} %get-tuple-element.45), custom_call_target="InvertDiagBlocksLowerTriangular" | custom-call | tf_op jit(solution)/shard_map/vmap(jit(cholesky))/cholesky | solution.py:9
  552.7 3.8 convolution_dynamic-update-slice_fusion
  556.5 6.8 slice_subtract_fusion.2
  564.1 59.4 %custom-call.80 = f32[5,128,128]{2,1,0:T(8,128)S(1)} custom-call(f32[5,128,128]{2,1,0:T(8,128)} %cholesky.592), custom_call_target="Cholesky" | custom-call | tf_op jit(solution)/shard_map/vmap(jit(cholesky))/cholesky | solution.py:9
  624.6 50.7 %custom-call.81 = f32[5,1,128,128]{2,3,1,0:T(8,128)} custom-call(f32[5,1,128,128]{3,2,1,0:T(8,128)} %get-tuple-element.43), custom_call_target="InvertDiagBlocksLowerTriangular" | custom-call | tf_op jit(solution)/shard_map/vmap(jit(cholesky))/cholesky | solution.py:9
  678.7 7.8 fusion.60
  687.2 59.4 %custom-call.82 = f32[5,128,128]{2,1,0:T(8,128)S(1)} custom-call(f32[5,128,128]{2,1,0:T(8,128)} %cholesky.597), custom_call_target="Cholesky" | custom-call | tf_op jit(solution)/shard_map/vmap(jit(cholesky))/cholesky | solution.py:9
  747.7 50.3 %custom-call.83 = f32[5,1,128,128]{2,3,1,0:T(8,128)S(1)} custom-call(f32[5,1,128,128]{3,2,1,0:T(8,128)} %get-tuple-element.41), custom_call_target="InvertDiagBlocksLowerTriangular" | custom-call | tf_op jit(solution)/shard_map/vmap(jit(cholesky))/cholesky | solution.py:9
  800.1 7.5 fusion.63
  807.7 58.6 %custom-call.84 = f32[5,128,128]{2,1,0:T(8,128)S(1)} custom-call(f32[5,128,128]{2,1,0:T(8,128)S(1)} %cholesky.602), custom_call_target="Cholesky" | custom-call | tf_op jit(solution)/shard_map/vmap(jit(cholesky))/cholesky | solution.py:9
  867.2 49.3 %custom-call.85 = f32[5,1,128,128]{2,3,1,0:T(8,128)S(1)} custom-call(f32[5,1,128,128]{3,2,1,0:T(8,128)S(1)} %get-tuple-element.39), custom_call_target="InvertDiagBlocksLowerTriangular" | custom-call | tf_op jit(solution)/shard_map/vmap(jit(cholesky))/cholesky | solution.py:9
  918.1 6.3 fusion.74
  925.2 60.1 %custom-call.86 = f32[5,128,128]{2,1,0:T(8,128)} custom-call(f32[5,128,128]{2,1,0:T(8,128)} %cholesky.607), custom_call_target="Cholesky" | custom-call | tf_op jit(solution)/shard_map/vmap(jit(cholesky))/cholesky | solution.py:9
  987.2 50.8 %custom-call.87 = f32[5,1,128,128]{2,3,1,0:T(8,128)} custom-call(f32[5,1,128,128]{3,2,1,0:T(8,128)} %get-tuple-element.37), custom_call_target="InvertDiagBlocksLowerTriangular" | custom-call | tf_op jit(solution)/shard_map/vmap(jit(cholesky))/cholesky | solution.py:9
  1040.2 4.8 fusion.79
  1045.0 58.6 %custom-call.88 = f32[5,128,128]{2,1,0:T(8,128)S(1)} custom-call(f32[5,128,128]{2,1,0:T(8,128)S(1)} %fusion.79), custom_call_target="Cholesky" | custom-call | tf_op jit(solution)/shard_map/vmap(jit(cholesky))/cholesky | solution.py:9
  1106.9 17.6 %select_select_fusion = f32[5,1024,1024]{2,1,0:T(8,128)} fusion(f32[5,1024,1024]{2,1,0:T(8,128)} %get-tuple-element.36, pred[5]{0:T(512)(128)(4,1)S(1)} %or_or_fusion, pred[1024,1024]{1,0:T(8,128)(4,1)S(1)} %copy-done.4), kind=kLoop, calls=%fused_computation.3 | loop fusion | flops 15728640 | bytes 42991620 | tf_op jit(solution)/shard_map/vmap(jit(_cho_solve))/triangular_solve | solution.py:10
  1124.5 31.4 %while.1 = (s32[]{:T(128)}, f32[5,1024,1024]{2,1,0:T(8,128)}, s32[8,2]{0,1:T(2,128)S(1)}, f32[8,5,128,128]{3,2,0,1:T(8,128)}, s32[]{:T(128)}) while((s32[]{:T(128)}, f32[5,1024,1024]{2,1,0:T(8,128)}, s32[8,2]{0,1:T(2,128)S(1)}, f32[8,5,128,128]{3,2,0,1:T(8,128)}, s32[]{:T(128)}) %tuple.69), condition=%wide.while_cond, body=%wide.while_body.sunk | while | flops 2 | bytes 656993 | solution.py:10
  1155.9 394.2 %custom-call.89 = f32[5,8,128,128]{2,3,1,0:T(8,128)S(1)} custom-call(f32[5,8,128,128]{3,2,1,0:T(8,128)} %bitcast.200), custom_call_target="InvertDiagBlocksLowerTriangular" | custom-call | tf_op jit(solution)/shard_map/vmap(jit(_cho_solve))/triangular_solve | solution.py:10
  1561.5 3.6 fusion.85
  1565.5 3.8 fusion.91
  1569.7 4.5 fusion.103
  1593.8 3.6 fusion.100
  1605.9 5.8 all-to-all-start
  1611.8 47.0 %all-to-all-done = bf16[1,64,5,4096]{3,2,0,1:T(8,128)(2,1)} async-done(((bf16[1,64,5,4096]{3,2,0,1:T(8,128)(2,1)}), bf16[1,64,5,4096]{3,2,0,1:T(8,128)(2,1)}, u32[]{:S(2)}, u32[]{:S(2)}) %all-to-all-start) | async-done | bytes 2621472 | tf_op jit(solution)/shard_map/all_to_all | solution.py:45
  1658.7 13.6 fusion.20
  1672.6 11.5 fusion.29
  1684.2 60.7 %all-reduce.1 = (f32[32,10,10]{0,2,1:T(8,128)S(1)}, f32[32,10]{0,1:T(8,128)S(1)}) all-reduce(f32[32,10,10]{0,2,1:T(8,128)S(1)} %reshape.170, f32[32,10]{0,1:T(8,128)S(1)} %reshape.171), channel_id=1, replica_groups=mesh['samp'=16,'blk'=2] {'samp'}, use_global_device_ids=true, to_apply=%region_22.23 | all-reduce | flops 3520 | bytes 28160 | tf_op jit(solution)/shard_map/psum | solution.py:48
  (152 shorter events, 102.8 us)
Async XLA Ops:
  7.2 138.3 %all-reduce.6.cloned.1.call-start = ((), (), s32[]{:S(2)}) async-start(), calls=%async_computation.1 | async-start | bytes 8912896 | tf_op jit(solution)/shard_map/psum | solution.py:32
  14.9 10.5 copy-start
  14.9 10.5 copy-start.3
  27.7 38.7 %copy-start.9 = (s32[5]{0:T(128)S(1)}, s32[5]{0:T(128)}, u32[]{:S(2)}) copy-start(s32[5]{0:T(128)} %param.5) | copy-start | bytes 64
  162.7 5.1 copy-start.2
  184.7 7.0 copy-start.1
  623.6 62.9 %copy-start.5 = (f32[5,128,128]{2,1,0:T(8,128)}, f32[5,128,128]{2,1,0:T(8,128)S(1)}, u32[]{:S(2)}) copy-start(f32[5,128,128]{2,1,0:T(8,128)S(1)} %custom-call.80) | copy-start | bytes 983044
  746.7 61.0 %copy-start.6 = (f32[5,128,128]{2,1,0:T(8,128)}, f32[5,128,128]{2,1,0:T(8,128)S(1)}, u32[]{:S(2)}) copy-start(f32[5,128,128]{2,1,0:T(8,128)S(1)} %custom-call.82) | copy-start | bytes 983044
  866.3 50.2 %copy-start.7 = (f32[5,128,128]{2,1,0:T(8,128)}, f32[5,128,128]{2,1,0:T(8,128)S(1)}, u32[]{:S(2)}) copy-start(f32[5,128,128]{2,1,0:T(8,128)S(1)} %custom-call.84) | copy-start | bytes 983044
  924.4 182.5 %copy-start.4 = (pred[1024,1024]{1,0:T(8,128)(4,1)S(1)}, pred[1024,1024]{1,0:T(8,128)(4,1)}, u32[]{:S(2)}) copy-start(pred[1024,1024]{1,0:T(8,128)(4,1)} %iota_compare_fusion.2) | copy-start | bytes 3145732
  1106.9 443.2 %copy-start.8 = (f32[1024,64]{0,1:T(8,128)S(1)}, f32[1024,64]{0,1:T(8,128)}, u32[]{:S(2)}) copy-start(f32[1024,64]{0,1:T(8,128)} %get-tuple-element.31) | copy-start | bytes 786436
  1589.7 9.5 slice-start
  1593.8 5.4 slice-start.1
  1605.9 52.8 %all-to-all-start = ((bf16[1,64,5,4096]{3,2,0,1:T(8,128)(2,1)}), bf16[1,64,5,4096]{3,2,0,1:T(8,128)(2,1)}, u32[]{:S(2)}, u32[]{:S(2)}) async-start(bf16[1,64,5,4096]{3,2,0,1:T(8,128)(2,1)} %copy.177), calls=%async_computation | async-start | bytes 8388608 | tf_op jit(solution)/shard_map/all_to_all | solution.py:45
Sparse Core Ops, SparseCore 0:
  27.8 117.5 all-reduce.5
where the time goes:
time: 1760 us; the launch traced here: 1750 us
  other arithmetic  1280 us (73%)
  matrix products  155 us (9%)
  waiting for transfers between devices  122 us (7%)
  blocking collectives  97.7 us (6%)
  local copies, waits for them, and re-layouts  78.8 us (4%)
    another operation x34, other arithmetic, ridge_solve(): factor = jnp.linalg.cholesky(gstd + penalty * eye)  836 us
    another operation x4, other arithmetic, ridge_solve(): return jax.scipy.linalg.cho_solve((factor, True), rhs)  413 us
    psum x1, waiting for transfers between devices, local(): lax.psum((gram_part, xty_part, col_part, ysum_part), 'samp')  74.7 us
    another operation x14, matrix products, ridge_solve(): factor = jnp.linalg.cholesky(gstd + penalty * eye)  65.6 us
    psum x1, blocking collectives, local(): level_gram, level_cross = lax.psum((gram_own, cross_own), 'samp')  60.7 us
    another operation x30, matrix products, ridge_solve(): return jax.scipy.linalg.cho_solve((factor, True), rhs)  47.3 us
    all_to_all x1, waiting for transfers between devices, local(): lax.all_to_all(pred[None], 'blk', split_axis=1, concat_axis=0, tiled=True)  47 us
    psum x1, blocking collectives, local(): lax.psum((gram_part, xty_part, col_part, ysum_part), 'samp')  37.1 us
  transfers between devices with their start and end apart: 2, of which 2 were waited for; matrix products, arithmetic and copies ran while one was open for 0% of the time, Pallas kernels for 0%

commit v1 on v0

v1 whole, which is shorter than its diff:
```python
import functools

import jax
import jax.numpy as jnp
from jax import lax
from jax.experimental import pallas as pl
from jax.experimental.pallas import tpu as pltpu
from jax.sharding import PartitionSpec as P

BLK = 128
SUB = 8
THIRD = 24
COPIES = 3
HI = lax.Precision.HIGHEST
NT = (((1,), (1,)), ((), ()))


def dot_hi(a, b):
    return jnp.dot(a, b, precision=HI, preferred_element_type=jnp.float32)


def dot_nt(a, b):
    return lax.dot_general(a, b, NT, precision=HI, preferred_element_type=jnp.float32)


def down(row):
    return jnp.transpose(jnp.broadcast_to(row, (BLK, BLK)))


def invert_tile(tile):
    strips = [tile[SUB * i:SUB * (i + 1), :] for i in range(BLK // SUB)]
    lane = lax.broadcasted_iota(jnp.int32, (SUB, BLK), 1)
    sub = lax.broadcasted_iota(jnp.int32, (SUB, BLK), 0)
    rows_at = [sub == j for j in range(SUB)]
    for k in range(BLK // SUB):
        at = SUB * k
        inside = (lane >= at) & (lane < at + SUB)
        eye = (lane - at == sub).astype(jnp.float32)
        cols = [jnp.broadcast_to(strips[k][:, at + j:at + j + 1], (SUB, BLK)) for j in range(SUB)]
        right = jnp.where(inside, eye, strips[k])
        for j in range(SUB):
            pivot = 1.0 / jnp.broadcast_to(cols[j][j:j + 1, :], (SUB, BLK))
            step = cols[j]

            def move(x):
                top = jnp.broadcast_to(x[j:j + 1, :], (SUB, BLK)) * pivot
                return jnp.where(rows_at[j], top, x - step * top)

            cols = cols[:j + 1] + [move(c) for c in cols[j + 1:]]
            right = move(right)
        tops = [jnp.broadcast_to(right[j:j + 1, :], (SUB, BLK)) for j in range(SUB)]
        fresh = []
        for i in range(BLK // SUB):
            if i == k:
                fresh.append(right)
                continue
            rest = jnp.where(inside, 0.0, strips[i])
            for j in range(SUB):
                rest = rest - jnp.broadcast_to(strips[i][:, at + j:at + j + 1], (SUB, BLK)) * tops[j]
            fresh.append(rest)
        strips = fresh
    return jnp.concatenate(strips, axis=0)


def solve_kernel(nsamp, ntraits, lam_ref, gram_ref, side_ref, coef_ref, aug, wide):
    nvars = gram_ref.shape[0]
    nblocks = nvars // BLK
    lam = lam_ref[0, 0]
    eye = lax.broadcasted_iota(jnp.int32, (BLK, BLK), 0) == lax.broadcasted_iota(jnp.int32, (BLK, BLK), 1)
    means, scales, means_down, scales_down = [], [], [], []
    for i in range(nblocks):
        span = slice(BLK * i, BLK * (i + 1))
        diag = jnp.sum(jnp.where(eye, gram_ref[span, span], 0.0), axis=0, keepdims=True)
        mean = side_ref[ntraits:ntraits + 1, span] / nsamp
        scale = 1.0 / jnp.sqrt(diag / nsamp - mean * mean + 1e-05)
        means.append(mean)
        scales.append(scale)
        means_down.append(down(mean))
        scales_down.append(down(scale))
    ysum = down(side_ref[ntraits + 1:ntraits + 2, 0:BLK])[0:ntraits, :]
    for j in range(nblocks):
        span = slice(BLK * j, BLK * (j + 1))
        for i in range(j, nblocks):
            rows = slice(BLK * i, BLK * (i + 1))
            value = gram_ref[rows, span] - nsamp * means_down[i] * means[j]
            value = value * (scales_down[i] * scales[j])
            if i == j:
                value = value + jnp.where(eye, lam, 0.0)
            aug[rows, span] = value
        aug[nvars:nvars + ntraits, span] = (side_ref[0:ntraits, span] - ysum * means[j]) * scales[j]
    end = nvars + ntraits

    def eliminate(k, carry):
        at = pl.multiple_of(k * BLK, BLK)
        inverse = invert_tile(aug[pl.ds(at, BLK), pl.ds(at, BLK)])
        for step in range(nblocks):
            @pl.when(k == step)
            def _(step=step):
                span = slice(BLK * step, BLK * (step + 1))
                low = BLK * (step + 1)
                panel = aug[low:end, span]
                mult = dot_hi(panel, inverse)
                wide[low:end, span] = mult
                for j in range(step + 1, nblocks):
                    top = BLK * j
                    aug[top:end, top:top + BLK] -= dot_nt(mult[top - low:, :], aug[top:top + BLK, span])
        return carry

    lax.fori_loop(0, nblocks, eliminate, 0)
    found = wide[nvars:end, nvars - BLK:nvars]
    solved = found
    parts = {nblocks - 1: found}
    for k in range(nblocks - 2, -1, -1):
        span = slice(BLK * k, BLK * (k + 1))
        found = wide[nvars:end, span] - dot_hi(solved, wide[BLK * (k + 1):nvars, span])
        parts[k] = found
        solved = jnp.concatenate([found, solved], axis=1)
    pad = coef_ref.shape[0] - ntraits
    for k in range(nblocks):
        span = slice(BLK * k, BLK * (k + 1))
        coef_ref[0:ntraits, span] = (parts[k] * scales[k]).astype(jnp.bfloat16)
        if pad > 0:
            coef_ref[ntraits:ntraits + pad, span] = jnp.zeros((pad, BLK), jnp.bfloat16)


def solve(gram, side, lam, nsamp, ntraits):
    nvars = gram.shape[0]
    return pl.pallas_call(
        functools.partial(solve_kernel, nsamp, ntraits),
        out_shape=jax.ShapeDtypeStruct((COPIES * THIRD, nvars), jnp.bfloat16),
        in_specs=[
            pl.BlockSpec(memory_space=pltpu.SMEM),
            pl.BlockSpec(memory_space=pltpu.VMEM),
            pl.BlockSpec(memory_space=pltpu.VMEM),
        ],
        out_specs=pl.BlockSpec(memory_space=pltpu.VMEM),
        scratch_shapes=[
            pltpu.VMEM((nvars + ntraits, nvars), jnp.float32),
            pltpu.VMEM((nvars + ntraits, nvars), jnp.float32),
        ],
        compiler_params=pltpu.CompilerParams(vmem_limit_bytes=48 * 1024 * 1024),
        cost_estimate=pl.CostEstimate(flops=100 * 10**9, bytes_accessed=200 * 10**6, transcendentals=0),
        name="ridge_solve",
    )(lam, gram, side)


def two_parts(value):
    first = value.astype(jnp.bfloat16)
    return first, (value - first.astype(jnp.float32)).astype(jnp.bfloat16)


def forms_kernel(nsamp, ntraits, npen, coef_ref, gram_ref, side_ref, cross_ref, out_ref, own, prod):
    nvars = gram_ref.shape[0]
    nblocks = nvars // BLK
    rank = lax.axis_index("blk")
    rows = COPIES * THIRD
    col_row = side_ref[ntraits:ntraits + 1, :]
    mean_own = col_row / nsamp
    mean_0 = cross_ref[nvars:nvars + 1, :] / nsamp
    mean_1 = cross_ref[nvars + 1:nvars + 2, :] / nsamp

    def at(r, q, b):
        return coef_ref[q * npen + r, b]

    def sheet(r, b):
        return jnp.concatenate([at(r, q, b) for q in range(COPIES)], axis=0)

    lane = lax.broadcasted_iota(jnp.int32, (rows, BLK), 1)
    acc = jnp.zeros((rows, BLK), jnp.float32)
    for r in range(npen):
        own[rows * r:rows * (r + 1), :] = jnp.concatenate([coef_ref[q * npen + r, rank] for q in range(COPIES)], axis=0).astype(jnp.float32)
    stack = own[...].astype(jnp.bfloat16)
    for j in range(0, nvars, 2 * BLK):
        span = slice(j, j + 2 * BLK)
        for i in range(0, nvars, 2 * BLK):
            tall = slice(i, i + 2 * BLK)
            down_mean = jnp.concatenate([down(mean_own[:, i:i + BLK]), down(mean_own[:, i + BLK:i + 2 * BLK])], axis=0)
            down_mean = jnp.concatenate([down_mean, down_mean], axis=1)
            value = gram_ref[tall, span] - nsamp * down_mean * mean_own[:, span]
            hi, lo = two_parts(value)
            part = jnp.dot(stack[:, tall], hi, preferred_element_type=jnp.float32)
            part = part + jnp.dot(stack[:, tall], lo, preferred_element_type=jnp.float32)
            if i == 0:
                prod[:, span] = part
            else:
                prod[:, span] += part
    place = 0
    for r in range(npen):
        for s in range(npen):
            if s < r:
                place += 1
                continue
            term = jnp.sum(prod[rows * r:rows * (r + 1), :] * own[rows * s:rows * (s + 1), :], axis=1, keepdims=True)
            acc = jnp.where((lane == place) | (lane == s * npen + r), term, acc)
            place += 1
    ysum = down(side_ref[ntraits + 1:ntraits + 2, 0:BLK])[0:ntraits, 0:1]
    target = side_ref[0:ntraits, :] - ysum * mean_own
    for r in range(npen):
        term = jnp.sum(own[rows * r:rows * r + ntraits, :] * target, axis=1, keepdims=True)
        term = jnp.concatenate([term, jnp.zeros((rows - ntraits, 1), jnp.float32)], axis=0)
        acc = jnp.where(lane == 2 * npen * npen + r, term, acc)
    for r in range(npen):
        own[rows * r:rows * (r + 1), :] = sheet(r, 1).astype(jnp.float32)
    stack = jnp.concatenate([sheet(r, 0) for r in range(npen)], axis=0)
    for j in range(0, nvars, 2 * BLK):
        span = slice(j, j + 2 * BLK)
        for i in range(0, nvars, 2 * BLK):
            tall = slice(i, i + 2 * BLK)
            down_mean = jnp.concatenate([down(mean_0[:, i:i + BLK]), down(mean_0[:, i + BLK:i + 2 * BLK])], axis=0)
            down_mean = jnp.concatenate([down_mean, down_mean], axis=1)
            value = cross_ref[tall, span] - nsamp * down_mean * mean_1[:, span]
            hi, lo = two_parts(value)
            part = jnp.dot(stack[:, tall], hi, preferred_element_type=jnp.float32)
            part = part + jnp.dot(stack[:, tall], lo, preferred_element_type=jnp.float32)
            if i == 0:
                prod[:, span] = part
            else:
                prod[:, span] += part
    place = npen * npen
    for r in range(npen):
        for s in range(npen):
            term = jnp.sum(prod[rows * r:rows * (r + 1), :] * own[rows * s:rows * (s + 1), :], axis=1, keepdims=True)
            acc = jnp.where(lane == place, term, acc)
            place += 1
    out_ref[...] = acc


def forms(coefs, gram, side, cross, nsamp, ntraits, npen):
    nvars = gram.shape[0]
    rows = COPIES * THIRD
    return pl.pallas_call(
        functools.partial(forms_kernel, nsamp, ntraits, npen),
        out_shape=jax.ShapeDtypeStruct((rows, BLK), jnp.float32),
        in_specs=[pl.BlockSpec(memory_space=pltpu.VMEM)] * 4,
        out_specs=pl.BlockSpec(memory_space=pltpu.VMEM),
        scratch_shapes=[
            pltpu.VMEM((npen * rows, nvars), jnp.float32),
            pltpu.VMEM((npen * rows, nvars), jnp.float32),
        ],
        compiler_params=pltpu.CompilerParams(vmem_limit_bytes=48 * 1024 * 1024),
        name="level_forms",
    )(coefs, gram, side, cross)


def sides(dosage, traits):
    ones = jnp.ones((traits.shape[0], 1), traits.dtype)
    pad = jnp.zeros((traits.shape[0], SUB - 1), traits.dtype)
    with_ones = jnp.concatenate([traits, ones, pad], axis=1)
    side = jnp.einsum("nt,nm->tm", with_ones, dosage, preferred_element_type=jnp.float32)
    ysum = jnp.sum(traits, axis=0, dtype=jnp.float32)
    ysum = jnp.pad(ysum, (0, dosage.shape[1] - ysum.shape[0]))
    return lax.dynamic_update_slice(side, ysum[None, :], (traits.shape[1] + 1, 0))


def gathered_order(coefs, npen, ntraits):
    coefs = coefs[:COPIES * npen].reshape(COPIES, npen, THIRD, coefs.shape[-1])
    coefs = coefs.transpose(1, 0, 2, 3).reshape(npen, COPIES * THIRD, coefs.shape[-1])
    return coefs[:, :ntraits]


def level_from_predictions(coefs, mean, dosage, traits, nvars):
    coef = coefs.transpose(0, 2, 1)
    ntraits = traits.shape[1]
    offset = jnp.einsum("rmt,m->rt", coef.astype(jnp.float32), mean, precision=HI)
    pred = jnp.einsum("rmt,nm->trn", coef, dosage, preferred_element_type=jnp.float32)
    pred = (pred - offset.T[:, :, None]).astype(jnp.bfloat16)
    local_traits = ntraits // lax.axis_size("blk")
    parts = lax.all_to_all(pred[None], "blk", split_axis=1, concat_axis=0, tiled=True)
    mine = lax.dynamic_slice_in_dim(traits, lax.axis_index("blk") * local_traits, local_traits, 1)
    gram = jnp.einsum("btrn,ctsn->tbrcs", parts, parts, preferred_element_type=jnp.float32)
    cross = jnp.einsum("btrn,nt->tbr", parts, mine, preferred_element_type=jnp.float32)
    count, stack = parts.shape[1], parts.shape[0] * parts.shape[2]
    gram, cross = lax.psum((gram.reshape(count, stack, stack), cross.reshape(count, stack)), "samp")
    return gram / nvars, cross / nvars


def local(genotypes, traits, penalty_index):
    dosage = genotypes.astype(jnp.bfloat16)
    count, nvars = dosage.shape
    ntraits = traits.shape[1]
    npen = penalty_index.shape[0]
    nblk = lax.axis_size("blk")
    nsamp = float(count * lax.axis_size("samp"))
    samp_rank = lax.axis_index("samp")
    blk_rank = lax.axis_index("blk")
    paired = nblk == 2
    if paired:
        half = count // 2
        sent = lax.dynamic_slice_in_dim(dosage, (1 - blk_rank) * half, half, 0)
        kept = lax.dynamic_slice_in_dim(dosage, blk_rank * half, half, 0)
        other = lax.ppermute(sent, "blk", [(0, 1), (1, 0)])
    gram = jnp.einsum("nm,nk->mk", dosage, dosage, preferred_element_type=jnp.float32)
    sums = lax.psum(jnp.concatenate([gram, sides(dosage, traits)], axis=0), "samp")
    gram, side = sums[:nvars], sums[nvars:]
    lam = nsamp * jnp.exp2((penalty_index.astype(jnp.float32) - 8.0) / 2.0)
    mine = lax.dynamic_index_in_dim(lam, samp_rank % npen, 0, keepdims=True).reshape(1, 1)
    coef = solve(gram, side, mine, nsamp, ntraits)
    third = lax.dynamic_slice_in_dim(coef, jnp.minimum(samp_rank // npen, COPIES - 1) * THIRD, THIRD, 0)
    if not paired:
        coefs = lax.all_gather(third, "samp")
        mean = side[ntraits] / nsamp
        return level_from_predictions(gathered_order(coefs, npen, ntraits), mean, dosage, traits, nvars)
    cross = jnp.einsum("nm,nk->mk", kept, other, preferred_element_type=jnp.float32)
    cross = jnp.where(blk_rank == 0, cross, cross.T)
    colsum = jnp.sum(dosage, axis=0, dtype=jnp.float32)
    tail = jnp.where(lax.broadcasted_iota(jnp.int32, (SUB, nvars), 0) == blk_rank, colsum[None, :], 0.0)
    cross = lax.psum(jnp.concatenate([cross, tail], axis=0), ("samp", "blk"))
    coefs = lax.all_gather(third, ("samp", "blk"))
    coefs = coefs.reshape(lax.axis_size("samp"), nblk, THIRD, nvars)
    found = forms(coefs, gram, side, cross, nsamp, ntraits, npen)[:ntraits] / nvars
    each = ntraits // nblk
    mixed = found[:, npen * npen:2 * npen * npen]
    mixed = lax.dynamic_slice_in_dim(mixed, blk_rank * each, each, 0).reshape(each, npen, npen)
    own = jnp.concatenate([found[:, :npen * npen], found[:, 2 * npen * npen:2 * npen * npen + npen]], axis=1)
    own = lax.all_to_all(own, "blk", split_axis=0, concat_axis=0, tiled=True)
    square = own[:, :npen * npen].reshape(nblk, each, npen, npen)
    upper = jnp.concatenate([square[0], mixed], axis=2)
    lower = jnp.concatenate([mixed.transpose(0, 2, 1), square[1]], axis=2)
    level_cross = own[:, npen * npen:].reshape(nblk, each, npen).transpose(1, 0, 2).reshape(each, nblk * npen)
    return jnp.concatenate([upper, lower], axis=1), level_cross


def solution(mesh):
    placed = (P("samp", "blk"), P("samp", None), P())
    return jax.shard_map(
        local,
        mesh=mesh,
        in_specs=placed,
        out_specs=(P("blk", None, None), P("blk", None)),
        check_vma=False,
    )
```

time: 1760 us -> 433 us (0.25)
  other arithmetic: 1280 us -> 20.9 us
  waiting for transfers between devices: 122 us -> 293 us
  matrix products: 155 us -> 22.3 us
  blocking collectives: 97.7 us -> 0 us
  local copies, waits for them, and re-layouts: 78.8 us -> 21.6 us
  Pallas kernels: 0 us -> 54.7 us
    another operation x38 -> x0, other arithmetic: 1250 us -> none  [the longest x34 836 us: ridge_solve(): factor = jnp.linalg.cholesky(gstd + penalty * eye)]
    psum x1 -> x2, waiting for transfers between devices: 74.7 us -> 256 us  [the longest x1 147 us: local(): cross = lax.psum(jnp.concatenate([cross, tail], axis=0), ('samp', 'blk'))]
    another operation x44 -> x0, matrix products: 113 us -> none  [the longest x14 65.6 us: ridge_solve(): factor = jnp.linalg.cholesky(gstd + penalty * eye)]
    psum x2 -> x0, blocking collectives: 97.7 us -> none  [the longest x1 60.7 us: local(): level_gram, level_cross = lax.psum((gram_own, cross_own), 'samp')]
    pallas_call x0 -> x2, Pallas kernels: none -> 54.7 us  [the longest x1 48.2 us: solve(): pl.pallas_call(functools.partial(solve_kernel, nsamp, ntraits), out_shape...]
    another operation x38 -> x0, local copies, waits for them, and re-layouts: 45 us -> none
    all_to_all x1, waiting for transfers between devices: 47 us -> 3.68 us  [local(): own = lax.all_to_all(own, 'blk', split_axis=0, concat_axis=0, tiled=True)]
    all_gather x0 -> x1, waiting for transfers between devices: none -> 32.4 us  [local(): coefs = lax.all_gather(third, ('samp', 'blk'))]
  transfers between devices with their start and end apart: 2 -> 5, of which waited for: 2 -> 4; matrix products, arithmetic and copies ran while one was open for 0% -> 7% of each run, Pallas kernels for 0% -> 11%
where the time goes in v1:
time: 433 us; the launch traced here: 432 us
  waiting for transfers between devices  293 us (68%)
  Pallas kernels  54.7 us (13%)
  matrix products  22.3 us (5%)
  local copies, waits for them, and re-layouts  21.6 us (5%)
  other arithmetic  20.9 us (5%)
  between operations  13.9 us (3%)
  starting transfers between devices  6.29 us (1%)
    psum x1, waiting for transfers between devices, local(): cross = lax.psum(jnp.concatenate([cross, tail], axis=0), ('samp', 'blk'))  147 us
    psum x1, waiting for transfers between devices, local(): lax.psum(jnp.concatenate([gram, sides(dosage, traits)], axis=0), 'samp')  109 us
    pallas_call x1, Pallas kernels, solve(): pl.pallas_call(functools.partial(solve_kernel, nsamp, ntraits), out_shape...  48.2 us
    all_gather x1, waiting for transfers between devices, local(): coefs = lax.all_gather(third, ('samp', 'blk'))  32.4 us
    dot_general x1, matrix products, local(): jnp.einsum('nm,nk->mk', dosage, dosage, preferred_element_type=jnp.float32)  10.5 us
    dot_general x1, matrix products, local(): jnp.einsum('nm,nk->mk', kept, other, preferred_element_type=jnp.float32)  10 us
  transfers between devices with their start and end apart: 5, of which 4 were waited for; matrix products, arithmetic and copies ran while one was open for 7% of the time, Pallas kernels for 11%

profile of v1, /device:TPU:0, one launch (start us, length us, event | category | flops | bytes accessed | tf_op | source)
XLA Modules:
  0.0 432.2 jit_solution(507303977926255718)
XLA Ops:
  7.2 0.0 all-reduce.4.cloned.1.call-start
  7.2 7.6 %convert_reduce_fusion = (f32[1024]{0:T(1024)S(1)}, bf16[4096,1024]{1,0:T(8,128)(2,1)S(1)}) fusion(s32[4096,1024]{1,0:T(8,128)} %param.3), kind=kLoop, calls=%fused_computation | loop fusion | flops 12581888 | bytes 25169920 | tf_op jit(solution)/shard_map/reduce_sum | solution.py:305
  14.9 10.5 %fusion.12 = f32[1024,1024]{1,0:T(8,128)} fusion(bf16[4096,1024]{1,0:T(8,128)(2,1)S(1)} %get-tuple-element.3), kind=kOutput, calls=%fused_computation.27 | convolution fusion | flops 8589934592 | bytes 12582912 | tf_op jit(solution)/shard_map/nm,nk->mk/dot_general | solution.py:292
  25.4 0.1 pad.17.clone
  25.5 0.1 pad.16.clone
  25.6 0.2 convert_reduce_fusion.1
  25.8 1.7 fusion.2
  27.5 0.1 dynamic_update_slice.3
  27.6 4.9 %pad_maximum_fusion = f32[1096,1024]{1,0:T(8,128)} fusion(f32[72,1024]{1,0:T(8,128)S(1)} %dynamic_update_slice.3, f32[1024,1024]{1,0:T(8,128)} %fusion.12), kind=kLoop, calls=%fused_computation.1 | loop fusion | flops 1122304 | bytes 8978432 | tf_op jit(solution)/shard_map/concatenate | solution.py:293
  32.5 0.0 all-reduce.4.cloned.1.call-update
  32.5 0.0 all-gather.3.cloned.1.call-start
  32.6 4.6 %constant_dynamic-slice_fusion.1 = bf16[2048,1024]{1,0:T(8,128)(2,1)} fusion(bf16[4096,1024]{1,0:T(8,128)(2,1)} %copy-done.3, s32[]{:T(128)S(6)} %select_n.45), kind=kLoop, calls=%fused_computation.19 | loop fusion | bytes 8388612 | tf_op jit(solution)/shard_map/dynamic_slice | solution.py:289
  37.2 2.9 collective-permute-start
  40.2 0.6 dynamic_slice.16
  40.8 108.9 %all-reduce.4.cloned.1.call-done = f32[1096,1024]{1,0:T(8,128)} async-done(((f32[1096,1024]{1,0:T(8,128)}), f32[1096,1024]{1,0:T(8,128)}) %all-reduce.4.cloned.1.call-update) | async-done | bytes 4489232 | tf_op jit(solution)/shard_map/psum | solution.py:293
  149.7 2.8 slice.41.gram_ref
  152.5 1.2 slice.42.side_ref
  153.7 48.2 %ridge_solve.1 = bf16[72,1024]{1,0:T(8,128)(2,1)S(1)} custom-call(f32[1,1]{1,0:T(1,128)} %bitcast.lam_ref, f32[1024,1024]{1,0:T(8,128)S(1)} %slice.41.gram_ref, f32[72,1024]{1,0:T(8,128)S(1)} %slice.42.side_ref), custom_call_target="tpu_custom_call" | custom-call | flops 99999997952 | bytes 200000000 | tf_op jit(solution)/shard_map/ridge_solve/pallas_call | solution.py:128
  201.9 0.6 constant_dynamic-slice_fusion.2
  202.5 0.0 all-gather.3.cloned.1.call-update
  202.5 0.0 all-reduce.6.cloned.1.call-start
  202.6 0.1 broadcast_select_fusion
  202.7 10.0 %fusion = f32[1024,1024]{1,0:T(8,128)} fusion(bf16[2048,1024]{1,0:T(8,128)(2,1)} %collective-permute-done, bf16[4096,1024]{1,0:T(8,128)(2,1)} %copy-done.3, s32[]{:T(128)S(6)} %select_n.44), kind=kOutput, calls=%fused_computation.4 | convolution fusion | flops 4294967296 | bytes 12582916 | tf_op jit(solution)/shard_map/nm,nk->mk/dot_general | solution.py:303
  212.7 5.4 %copy.8 = f32[1024,1024]{0,1:T(8,128)} copy(f32[1024,1024]{1,0:T(8,128)} %fusion) | data formatting | bytes 8388608 | tf_op jit(solution)/shard_map/nm,nk->mk/dot_general | solution.py:303
  218.1 4.4 %bitcast_select_fusion = f32[1024,1024]{1,0:T(8,128)S(1)} fusion(f32[1024,1024]{1,0:T(8,128)} %fusion, f32[1024,1024]{0,1:T(8,128)} %copy.8, pred[]{:T(512)S(6)} %eq.12), kind=kLoop, calls=%fused_computation.3 | loop fusion | flops 1048576 | bytes 12582913 | tf_op jit(solution)/shard_map/jit(_where)/select_n | solution.py:304
  222.5 2.3 pad_maximum_fusion.1
  224.8 0.0 all-reduce.6.cloned.1.call-update
  224.8 32.4 %all-gather.3.cloned.1.call-done = bf16[768,1024]{1,0:T(8,128)(2,1)} async-done(((bf16[24,1024]{1,0:T(8,128)(2,1)}), bf16[768,1024]{1,0:T(8,128)(2,1)}) %all-gather.3.cloned.1.call-update) | async-done | bytes 1572880 | tf_op jit(solution)/shard_map/all_gather | solution.py:308
  257.2 147.5 %all-reduce.6.cloned.1.call-done.cross_ref = f32[1032,1024]{1,0:T(8,128)} async-done(((f32[1032,1024]{1,0:T(8,128)}), f32[1032,1024]{1,0:T(8,128)}) %all-reduce.6.cloned.1.call-update) | async-done | bytes 4227088 | tf_op jit(solution)/shard_map/psum | solution.py:307
  404.7 2.2 copy-done.1
  406.9 1.4 copy-done.2
  408.3 6.5 %level_forms.1 = f32[72,128]{1,0:T(8,128)S(1)} custom-call(bf16[16,2,24,1024]{3,2,1,0:T(8,128)(2,1)S(1)} %bitcast.25, f32[1024,1024]{1,0:T(8,128)S(1)} %copy-done.1, f32[72,1024]{1,0:T(8,128)S(1)} %slice.42.side_ref, f32[1032,1024]{1,0:T(8,128)} %all-reduce.6.cloned.1.call-done.cross_ref), custom_call_target="tpu_custom_call" | custom-call | tf_op jit(solution)/shard_map/level_forms/pallas_call | solution.py:231
  414.8 0.1 fusion.11
  414.8 0.1 slice.45
  414.9 0.1 pad_maximum_fusion.2
  415.0 0.7 reshape.35
  415.7 3.2 all-to-all-start
  419.0 0.1 copy.10
  419.1 3.7 all-to-all-done
  422.8 0.5 broadcast.31
  423.3 0.7 reduce
  423.9 0.1 reshape.36
  424.1 0.1 slice.49
  424.1 0.1 copy.14
  424.2 0.1 copy.15
  424.3 0.1 copy.17
  424.4 0.6 reshape.31
  425.0 0.7 maximum_maximum_fusion
  (23 shorter events, 0.1 us)
Async XLA Ops:
  7.2 142.6 %all-reduce.4.cloned.1.call-start = ((), (), s32[]{:S(2)}) async-start(), calls=%async_computation.1 | async-start | bytes 8978432 | tf_op jit(solution)/shard_map/psum | solution.py:293
  14.9 10.9 %copy-start.3 = (bf16[4096,1024]{1,0:T(8,128)(2,1)}, bf16[4096,1024]{1,0:T(8,128)(2,1)S(1)}, u32[]{:S(2)}) copy-start(bf16[4096,1024]{1,0:T(8,128)(2,1)S(1)} %get-tuple-element.3) | copy-start | bytes 25165828
  14.9 10.7 %copy-start.4 = (bf16[4096,64]{0,1:T(8,128)(2,1)S(1)}, bf16[4096,64]{0,1:T(8,128)(2,1)}, u32[]{:S(2)}) copy-start(bf16[4096,64]{0,1:T(8,128)(2,1)} %param.4) | copy-start | bytes 1572868
  32.5 7.7 %copy-start.5 = (s32[5]{0:T(128)S(1)}, s32[5]{0:T(128)}, u32[]{:S(2)}) copy-start(s32[5]{0:T(128)} %param.5) | copy-start | bytes 64
  32.5 224.7 %all-gather.3.cloned.1.call-start = ((), (), s32[]{:S(2)}) async-start(), calls=%async_computation.3 | async-start | bytes 1622016 | tf_op jit(solution)/shard_map/all_gather | solution.py:308
  37.2 165.4 %collective-permute-start = (bf16[2048,1024]{1,0:T(8,128)(2,1)}, bf16[2048,1024]{1,0:T(8,128)(2,1)}, u32[]{:S(2)}, u32[]{:S(2)}) collective-permute-start(bf16[2048,1024]{1,0:T(8,128)(2,1)} %constant_dynamic-slice_fusion.1), channel_id=1, source_target_pairs={{0,1},{1,0},{2,3},{3,2},{4,5},{5,4},{6,7},{7,6},{8,9},{9,8},{10,11... | collective-permute-start | bytes 12582920 | tf_op jit(solution)/shard_map/ppermute | solution.py:291
  152.5 49.4 %copy-start = (f32[1024,1024]{1,0:T(8,128)}, f32[1024,1024]{1,0:T(8,128)S(1)}, u32[]{:S(2)}) copy-start(f32[1024,1024]{1,0:T(8,128)S(1)} %slice.41.gram_ref) | copy-start | bytes 12582916
  202.5 202.1 %all-reduce.6.cloned.1.call-start = ((), (), s32[]{:S(2)}) async-start(), calls=%async_computation.2 | async-start | bytes 8454144 | tf_op jit(solution)/shard_map/psum | solution.py:307
  404.7 2.2 copy-start.1
  406.9 1.4 copy-start.2
  415.7 7.0 %all-to-all-start = ((f32[2,1,960]{2,1,0:T(1,128)}), f32[2,1,960]{2,1,0:T(1,128)S(1)}, u32[]{:S(2)}, u32[]{:S(2)}) async-start(f32[2,1,960]{2,1,0:T(1,128)} %reshape.35), calls=%async_computation | async-start | bytes 16384 | tf_op jit(solution)/shard_map/all_to_all | solution.py:315
Sparse Core Ops, SparseCore 0:
  32.6 117.0 all-reduce.3
  202.6 54.5 all-gather.2
  262.9 141.7 all-reduce.5

commit v2 on v0

v2 whole, which is shorter than its diff:
```python
import functools

import jax
import jax.numpy as jnp
from jax import lax
from jax.experimental import pallas as pl
from jax.experimental.pallas import tpu as pltpu
from jax.sharding import PartitionSpec as P

BLK = 128
SUB = 8
GROUP = 8
HI = lax.Precision.HIGHEST
NT = (((1,), (1,)), ((), ()))
TN = (((0,), (0,)), ((), ()))


def dot_hi(a, b):
    return jnp.dot(a, b, precision=HI, preferred_element_type=jnp.float32)


def dot_nt(a, b):
    return lax.dot_general(a, b, NT, precision=HI, preferred_element_type=jnp.float32)


def panel_rows(nvars):
    starts = [0]
    for j in range(nvars // BLK):
        starts.append(starts[-1] + nvars - BLK * j)
    return starts[:-1], starts[-1]


def side_rows(ntraits):
    return ntraits + SUB


def down(row):
    return jnp.transpose(jnp.broadcast_to(row, (BLK, BLK)))


def invert_tile(tile):
    strips = [tile[SUB * i:SUB * (i + 1), :] for i in range(BLK // SUB)]
    lane = lax.broadcasted_iota(jnp.int32, (SUB, BLK), 1)
    sub = lax.broadcasted_iota(jnp.int32, (SUB, BLK), 0)
    rows_at = [sub == j for j in range(SUB)]
    for k in range(BLK // SUB):
        at = SUB * k
        inside = (lane >= at) & (lane < at + SUB)
        eye = (lane - at == sub).astype(jnp.float32)
        cols = [jnp.broadcast_to(strips[k][:, at + j:at + j + 1], (SUB, BLK)) for j in range(SUB)]
        right = jnp.where(inside, eye, strips[k])
        for j in range(SUB):
            pivot = 1.0 / jnp.broadcast_to(cols[j][j:j + 1, :], (SUB, BLK))
            step = cols[j]

            def move(x):
                top = jnp.broadcast_to(x[j:j + 1, :], (SUB, BLK)) * pivot
                return jnp.where(rows_at[j], top, x - step * top)

            cols = cols[:j + 1] + [move(c) for c in cols[j + 1:]]
            right = move(right)
        tops = [jnp.broadcast_to(right[j:j + 1, :], (SUB, BLK)) for j in range(SUB)]
        fresh = []
        for i in range(BLK // SUB):
            if i == k:
                fresh.append(right)
                continue
            rest = jnp.where(inside, 0.0, strips[i])
            for j in range(SUB):
                rest = rest - jnp.broadcast_to(strips[i][:, at + j:at + j + 1], (SUB, BLK)) * tops[j]
            fresh.append(rest)
        strips = fresh
    return jnp.concatenate(strips, axis=0)


def gram_kernel(ntraits, rank_ref, geno_ref, traits_ref, packed_ref, sent_ref, kept_ref, side, *panels):
    nvars = geno_ref.shape[1]
    step = pl.program_id(0)
    half = pl.num_programs(0) // 2
    wide = 2 * BLK

    @pl.when(step == 0)
    def _():
        side[...] = jnp.zeros_like(side)
        for panel in panels:
            panel[...] = jnp.zeros_like(panel)

    dosage = geno_ref[...].astype(jnp.float32).astype(jnp.bfloat16)

    @pl.when(step < half)
    def _():
        sent_ref[...] = dosage

    @pl.when(step >= half)
    def _():
        kept_ref[...] = dosage

    turned = jnp.transpose(dosage)
    for j, panel in enumerate(panels):
        panel[...] += jnp.dot(turned[wide * j:, :], dosage[:, wide * j:wide * (j + 1)], preferred_element_type=jnp.float32)
    traits = traits_ref[...]
    side[0:ntraits, :] += lax.dot_general(traits, dosage, TN, preferred_element_type=jnp.float32)
    ones = jnp.ones((SUB, dosage.shape[0]), jnp.bfloat16)
    sums = jnp.dot(ones, dosage, preferred_element_type=jnp.float32)
    ysum = jnp.dot(ones, traits, preferred_element_type=jnp.float32)
    ysum = jnp.concatenate([ysum, jnp.zeros((SUB, BLK - ntraits), jnp.float32)], axis=1)
    ysum = jnp.concatenate([ysum, jnp.zeros((SUB, nvars - BLK), jnp.float32)], axis=1)
    row = lax.broadcasted_iota(jnp.int32, (SUB, nvars), 0)
    side[ntraits:ntraits + SUB, :] += jnp.where(row == 0, sums, jnp.where(row == 1, ysum, 0.0))

    @pl.when(step == pl.num_programs(0) - 1)
    def _():
        starts, low = panel_rows(nvars)
        for j, start in enumerate(starts):
            panel = panels[j // 2]
            skip = BLK * (j % 2)
            packed_ref[start:start + nvars - BLK * j, :] = panel[skip:, skip:skip + BLK]
        tall = side_rows(ntraits)
        for j in range(nvars // BLK):
            packed_ref[low + tall * j:low + tall * (j + 1), :] = side[:, BLK * j:BLK * (j + 1)]


def gram(genotypes, traits, rank):
    count, nvars = genotypes.shape
    ntraits = traits.shape[1]
    steps = 8
    tile = count // steps
    half = steps // 2
    low = panel_rows(nvars)[1]
    total = low + side_rows(ntraits) * (nvars // BLK)

    def source(i, rank_ref):
        return (lax.rem(i + half * (1 - rank_ref[0]), steps), 0)

    halves = jax.ShapeDtypeStruct((count // 2, nvars), jnp.bfloat16)
    return pl.pallas_call(
        functools.partial(gram_kernel, ntraits),
        grid_spec=pltpu.PrefetchScalarGridSpec(
            num_scalar_prefetch=1,
            grid=(steps,),
            in_specs=[pl.BlockSpec((tile, nvars), source), pl.BlockSpec((tile, ntraits), source)],
            out_specs=[
                pl.BlockSpec((total, BLK), lambda i, rank_ref: (0, 0)),
                pl.BlockSpec((tile, nvars), lambda i, rank_ref: (jnp.minimum(i, half - 1), 0)),
                pl.BlockSpec((tile, nvars), lambda i, rank_ref: (jnp.maximum(i - half, 0), 0)),
            ],
            scratch_shapes=[pltpu.VMEM((side_rows(ntraits), nvars), jnp.float32)]
            + [pltpu.VMEM((nvars - 2 * BLK * j, 2 * BLK), jnp.float32) for j in range(nvars // (2 * BLK))],
        ),
        out_shape=[jax.ShapeDtypeStruct((total, BLK), jnp.float32), halves, halves],
        compiler_params=pltpu.CompilerParams(vmem_limit_bytes=48 * 1024 * 1024),
        name="gram_sums",
    )(rank.reshape(1), genotypes, traits)


def solve_kernel(nsamp, ntraits, lam_ref, packed_ref, coef_ref, aug, wide):
    nvars = coef_ref.shape[1]
    nblocks = nvars // BLK
    starts, low = panel_rows(nvars)
    tall = side_rows(ntraits)
    lam = lam_ref[0, 0]
    eye = lax.broadcasted_iota(jnp.int32, (BLK, BLK), 0) == lax.broadcasted_iota(jnp.int32, (BLK, BLK), 1)
    sides = [packed_ref[low + tall * j:low + tall * (j + 1), :] for j in range(nblocks)]
    means = [side[ntraits:ntraits + 1, :] / nsamp for side in sides]
    means_down = [down(mean) for mean in means]
    ysum = down(sides[0][ntraits + 1:ntraits + 2, :])[0:ntraits, :]
    for j in range(nblocks):
        span = slice(BLK * j, BLK * (j + 1))
        for i in range(j, nblocks):
            at = starts[j] + BLK * (i - j)
            value = packed_ref[at:at + BLK, :] - nsamp * means_down[i] * means[j]
            if i == j:
                value = value + jnp.where(eye, lam * (value / nsamp + 1e-05), 0.0)
            aug[BLK * i:BLK * (i + 1), span] = value
        aug[nvars:nvars + ntraits, span] = sides[j][0:ntraits, :] - ysum * means[j]
    end = nvars + ntraits

    def eliminate(k, carry):
        at = pl.multiple_of(k * BLK, BLK)
        inverse = invert_tile(aug[pl.ds(at, BLK), pl.ds(at, BLK)])
        for step in range(nblocks):
            @pl.when(k == step)
            def _(step=step):
                span = slice(BLK * step, BLK * (step + 1))
                first = BLK * (step + 1)
                mult = dot_hi(aug[first:end, span], inverse)
                wide[first:end, span] = mult
                for j in range(step + 1, nblocks):
                    top = BLK * j
                    aug[top:end, top:top + BLK] -= dot_nt(mult[top - first:, :], aug[top:top + BLK, span])
        return carry

    lax.fori_loop(0, nblocks, eliminate, 0)
    solved = wide[nvars:end, nvars - BLK:nvars]
    coef_ref[:, nvars - BLK:nvars] = solved.astype(jnp.bfloat16)
    for k in range(nblocks - 2, -1, -1):
        span = slice(BLK * k, BLK * (k + 1))
        found = wide[nvars:end, span] - dot_hi(solved, wide[BLK * (k + 1):nvars, span])
        coef_ref[:, span] = found.astype(jnp.bfloat16)
        solved = jnp.concatenate([found, solved], axis=1)


def solve(packed, lam, nsamp, nvars, ntraits):
    return pl.pallas_call(
        functools.partial(solve_kernel, nsamp, ntraits),
        out_shape=jax.ShapeDtypeStruct((ntraits, nvars), jnp.bfloat16),
        in_specs=[pl.BlockSpec(memory_space=pltpu.SMEM), pl.BlockSpec(memory_space=pltpu.VMEM)],
        out_specs=pl.BlockSpec(memory_space=pltpu.VMEM),
        scratch_shapes=[
            pltpu.VMEM((nvars + ntraits, nvars), jnp.float32),
            pltpu.VMEM((nvars + ntraits, nvars), jnp.float32),
        ],
        compiler_params=pltpu.CompilerParams(vmem_limit_bytes=48 * 1024 * 1024),
        cost_estimate=pl.CostEstimate(flops=50 * 10**9, bytes_accessed=20 * 10**6, transcendentals=0),
        name="ridge_solve",
    )(lam, packed)


def level_kernel(npen, own_ref, other_ref, coef_ref, mean_ref, traits_ref, out_ref, pred):
    rank = lax.axis_index("blk")
    ntraits = coef_ref.shape[2]
    nvars = own_ref.shape[1]
    count = own_ref.shape[0]
    stack = 2 * npen
    tile = 512
    for place in range(2):
        block = rank if place == 0 else 1 - rank
        source = own_ref if place == 0 else other_ref
        mean = mean_ref[pl.ds(block, 1), :]
        coef = jnp.concatenate([coef_ref[r, block] for r in range(npen)], axis=0)
        offset = jnp.sum(coef.astype(jnp.float32) * mean, axis=1, keepdims=True)
        low = pl.multiple_of(block * (npen * ntraits), npen * ntraits)
        for n in range(0, count, tile):
            value = lax.dot_general(coef, source[n:n + tile, :], NT, preferred_element_type=jnp.float32)
            pred[pl.ds(low, npen * ntraits), n:n + tile] = value - offset
    for n in range(0, count, tile):
        rows = traits_ref[n:n + tile, :].astype(jnp.float32)
        rows = jnp.concatenate([rows, jnp.zeros((tile, BLK - ntraits), jnp.float32)], axis=1)
        pred[stack * ntraits:(stack + 1) * ntraits, n:n + tile] = jnp.transpose(rows)[0:ntraits, :]
    lane = lax.broadcasted_iota(jnp.int32, (SUB, BLK), 1)
    for t in range(0, ntraits, SUB):
        acc = jnp.zeros((SUB, BLK), jnp.float32)
        for i in range(stack):
            left = pred[i * ntraits + t:i * ntraits + t + SUB, :]
            for j in range(i, stack + 1):
                term = jnp.sum(left * pred[j * ntraits + t:j * ntraits + t + SUB, :], axis=1, keepdims=True)
                if j < stack:
                    acc = jnp.where((lane == i * stack + j) | (lane == j * stack + i), term, acc)
                else:
                    acc = jnp.where(lane == stack * stack + i, term, acc)
        out_ref[t:t + SUB, :] = acc


def level_sums(own, other, coefs, means, traits, npen):
    ntraits = traits.shape[1]
    count = own.shape[0]
    return pl.pallas_call(
        functools.partial(level_kernel, npen),
        out_shape=jax.ShapeDtypeStruct((ntraits, BLK), jnp.float32),
        in_specs=[pl.BlockSpec(memory_space=pltpu.VMEM)] * 5,
        out_specs=pl.BlockSpec(memory_space=pltpu.VMEM),
        scratch_shapes=[pltpu.VMEM(((2 * npen + 1) * ntraits, count), jnp.float32)],
        compiler_params=pltpu.CompilerParams(vmem_limit_bytes=56 * 1024 * 1024),
        name="level_sums",
    )(own, other, coefs, means, traits)


def level_from_predictions(coefs, mean, dosage, traits, nvars):
    coef = coefs.transpose(0, 2, 1)
    ntraits = traits.shape[1]
    offset = jnp.einsum("rmt,m->rt", coef.astype(jnp.float32), mean, precision=HI)
    pred = jnp.einsum("rmt,nm->trn", coef, dosage, preferred_element_type=jnp.float32)
    pred = (pred - offset.T[:, :, None]).astype(jnp.bfloat16)
    local_traits = ntraits // lax.axis_size("blk")
    parts = lax.all_to_all(pred[None], "blk", split_axis=1, concat_axis=0, tiled=True)
    mine = lax.dynamic_slice_in_dim(traits, lax.axis_index("blk") * local_traits, local_traits, 1)
    gram = jnp.einsum("btrn,ctsn->tbrcs", parts, parts, preferred_element_type=jnp.float32)
    cross = jnp.einsum("btrn,nt->tbr", parts, mine, preferred_element_type=jnp.float32)
    count, stack = parts.shape[1], parts.shape[0] * parts.shape[2]
    gram, cross = lax.psum((gram.reshape(count, stack, stack), cross.reshape(count, stack)), "samp")
    return gram / nvars, cross / nvars


def local(genotypes, traits, penalty_index):
    count, nvars = genotypes.shape
    ntraits = traits.shape[1]
    npen = penalty_index.shape[0]
    nblk = lax.axis_size("blk")
    members = lax.axis_size("samp")
    nsamp = float(count * members)
    samp_rank = lax.axis_index("samp")
    blk_rank = lax.axis_index("blk")
    paired = nblk == 2
    packed, sent, kept = gram(genotypes, traits, blk_rank if paired else jnp.int32(0))
    if paired:
        other = lax.ppermute(sent, "blk", [(0, 1), (1, 0)])
    sums = lax.psum(packed, "samp")
    low = panel_rows(nvars)[1]
    tall = side_rows(ntraits)
    mean = jnp.concatenate([sums[low + tall * j + ntraits] for j in range(nvars // BLK)]) / nsamp
    lam = nsamp * jnp.exp2((penalty_index.astype(jnp.float32) - 8.0) / 2.0)
    mine = lax.dynamic_index_in_dim(lam, (samp_rank % GROUP) % npen, 0, keepdims=True).reshape(1, 1)
    coef = solve(sums, mine, nsamp, nvars, ntraits)
    groups = [list(range(g, g + GROUP)) for g in range(0, members, GROUP)]
    if not paired:
        coefs = lax.all_gather(coef, "samp", axis_index_groups=groups)[:npen]
        dosage = genotypes.astype(jnp.bfloat16)
        return level_from_predictions(coefs, mean, dosage, traits, nvars)
    mean_far = lax.ppermute(mean, "blk", [(0, 1), (1, 0)])
    coef_far = lax.ppermute(coef, "blk", [(0, 1), (1, 0)])
    first = blk_rank == 0
    means = jnp.stack([jnp.where(first, mean, mean_far), jnp.where(first, mean_far, mean)])
    both = jnp.stack([jnp.where(first, coef, coef_far), jnp.where(first, coef_far, coef)])
    coefs = lax.all_gather(both, "samp", axis_index_groups=groups)
    rows = lax.dynamic_slice_in_dim(traits, blk_rank * (count // 2), count // 2, 0)
    found = level_sums(kept, other, coefs, means, rows, npen)
    stack = nblk * npen
    found = lax.psum(found, ("samp", "blk")) / nvars
    each = ntraits // nblk
    found = lax.dynamic_slice_in_dim(found, blk_rank * each, each, 0)
    return found[:, :stack * stack].reshape(each, stack, stack), found[:, stack * stack:stack * stack + stack]


def solution(mesh):
    placed = (P("samp", "blk"), P("samp", None), P())
    return jax.shard_map(
        local,
        mesh=mesh,
        in_specs=placed,
        out_specs=(P("blk", None, None), P("blk", None)),
        check_vma=False,
    )
```

time: 1760 us -> 267 us (0.15)
  other arithmetic: 1280 us -> 1.39 us
  matrix products: 155 us -> 0 us
  Pallas kernels: 0 us -> 74.7 us
  local copies, waits for them, and re-layouts: 78.8 us -> 13.2 us
  blocking collectives: 97.7 us -> 40.5 us
    another operation x38 -> x3, other arithmetic: 1250 us -> 1.36 us  [the longest x2 0.74 us: local(): jnp.stack([jnp.where(first, coef, coef_far), jnp.where(first, coef_far, c...]
    another operation x44 -> x0, matrix products: 113 us -> none  [the longest x14 65.6 us: ridge_solve(): factor = jnp.linalg.cholesky(gstd + penalty * eye)]
    pallas_call x0 -> x3, Pallas kernels: none -> 74.7 us  [the longest x1 47.8 us: solve(): pl.pallas_call(functools.partial(solve_kernel, nsamp, ntraits), out_shape...]
    psum x2 -> x1, blocking collectives: 97.7 us -> 40.5 us  [local(): found = lax.psum(found, ('samp', 'blk')) / nvars]
    all_to_all x1 -> x0, waiting for transfers between devices: 47 us -> none  [local(): lax.all_to_all(pred[None], 'blk', split_axis=1, concat_axis=0, tiled=True)]
    another operation x38 -> x0, local copies, waits for them, and re-layouts: 45 us -> none
    dot_general x6 -> x0, matrix products: 41.9 us -> none  [the longest x1 13.6 us: level_sums(): jnp.einsum('btrn,ctsn->tbrcs', parts, parts, preferred_element_type=jnp.f...]
    psum x1, waiting for transfers between devices: 74.7 us -> 100 us  [local(): sums = lax.psum(packed, 'samp')]
  transfers between devices with their start and end apart: 2 -> 5, of which waited for: 2 -> 4; matrix products, arithmetic and copies ran while one was open for 0% -> 3% of each run, Pallas kernels for 0% -> 18%
where the time goes in v2:
time: 267 us; the launch traced here: 266 us
  waiting for transfers between devices  116 us (43%)
  Pallas kernels  74.7 us (28%)
  blocking collectives  40.5 us (15%)
  between operations  14.1 us (5%)
  local copies, waits for them, and re-layouts  13.2 us (5%)
  starting transfers between devices  6.1 us (2%)
    psum x1, waiting for transfers between devices, local(): sums = lax.psum(packed, 'samp')  100 us
    pallas_call x1, Pallas kernels, solve(): pl.pallas_call(functools.partial(solve_kernel, nsamp, ntraits), out_shape...  47.8 us
    psum x1, blocking collectives, local(): found = lax.psum(found, ('samp', 'blk')) / nvars  40.5 us
    pallas_call x1, Pallas kernels, gram(): pl.pallas_call(functools.partial(gram_kernel, ntraits), grid_spec=pltpu.P...  16.9 us
    all_gather x1, waiting for transfers between devices, local(): coefs = lax.all_gather(both, 'samp', axis_index_groups=groups)  11.1 us
    unnamed x15, local copies, waits for them, and re-layouts  10.2 us
    pallas_call x1, Pallas kernels, level_sums(): pl.pallas_call(functools.partial(level_kernel, npen), out_shape=jax.Shape...  9.95 us
  transfers between devices with their start and end apart: 5, of which 4 were waited for; matrix products, arithmetic and copies ran while one was open for 3% of the time, Pallas kernels for 18%

profile of v2, /device:TPU:0, one launch (start us, length us, event | category | flops | bytes accessed | tf_op | source)
XLA Modules:
  0.0 265.9 jit_solution(12775512939824042334)
XLA Ops:
  7.2 0.0 all-reduce.2.cloned.1.call-start
  7.2 1.5 copy.13.traits_ref
  8.7 16.9 %gram_sums.1 = (f32[5184,128]{1,0:T(8,128)S(1)}, bf16[2048,1024]{1,0:T(8,128)(2,1)}, bf16[2048,1024]{1,0:T(8,128)(2,1)}) custom-call(s32[1]{0:T(128)} %bitcast.rank_ref, s32[4096,1024]{1,0:T(8,128)} %geno_ref.1, bf16[4096,64]{1,0:T(8,128)(2,1)S(1)} %copy.13.traits_ref), custom_call_target="tpu_custom_call" | custom-call | tf_op jit(solution)/shard_map/gram_sums/pallas_call | solution.py:136
  25.7 0.0 copy-start
  25.7 1.5 copy-done
  27.1 0.0 copy-start.2
  27.1 0.0 all-reduce.2.cloned.1.call-update
  27.2 0.0 all-gather.3.cloned.1.call-start
  27.2 3.0 %collective-permute-start = (bf16[2048,1024]{1,0:T(8,128)(2,1)}, bf16[2048,1024]{1,0:T(8,128)(2,1)}, u32[]{:S(2)}, u32[]{:S(2)}) collective-permute-start(bf16[2048,1024]{1,0:T(8,128)(2,1)} %get-tuple-element.6), channel_id=1, source_target_pairs={{0,1},{1,0},{2,3},{3,2},{4,5},{5,4},{6,7},{7,6},{8,9},{9,8},{10,11... | collective-permute-start | bytes 12582920 | tf_op jit(solution)/shard_map/ppermute | solution.py:296
  30.2 0.0 copy-done.2
  30.2 0.6 dynamic_slice.10
  30.8 100.0 %all-reduce.2.cloned.1.call-done.packed_ref = f32[5184,128]{1,0:T(8,128)} async-done(((f32[5184,128]{1,0:T(8,128)}), f32[5184,128]{1,0:T(8,128)}) %all-reduce.2.cloned.1.call-update) | async-done | bytes 2654224 | tf_op jit(solution)/shard_map/psum | solution.py:297
  130.8 0.0 copy-start.1
  130.8 1.7 copy-done.1
  132.6 47.8 %ridge_solve.1 = bf16[64,1024]{1,0:T(8,128)(2,1)S(1)} custom-call(f32[1,1]{1,0:T(1,128)} %bitcast.1.lam_ref, f32[5184,128]{1,0:T(8,128)S(1)} %copy-done.1), custom_call_target="tpu_custom_call" | custom-call | flops 49999998976 | bytes 20000000 | tf_op jit(solution)/shard_map/ridge_solve/pallas_call | solution.py:204
  180.4 1.5 collective-permute-start.1
  181.9 3.5 %collective-permute-done.1 = bf16[64,1024]{1,0:T(8,128)(2,1)S(1)} collective-permute-done((bf16[64,1024]{1,0:T(8,128)(2,1)S(1)}, bf16[64,1024]{1,0:T(8,128)(2,1)S(1)}, u32[]{:S(2)}, u32[]{:S(2)}) %collective-permute-start.1) | collective-permute-done | bytes 131104 | tf_op jit(solution)/shard_map/ppermute | solution.py:310
  185.5 0.7 pad_maximum_fusion
  186.2 0.0 all-gather.3.cloned.1.call-update
  186.2 0.7 constant_dynamic-update-slice_fusion.7
  186.9 0.7 constant_dynamic-update-slice_fusion.6
  187.6 0.7 constant_dynamic-update-slice_fusion.5
  188.3 0.7 constant_dynamic-update-slice_fusion.4
  189.0 0.7 constant_dynamic-update-slice_fusion.3
  189.6 0.7 constant_dynamic-update-slice_fusion.2
  190.3 0.7 constant_dynamic-update-slice_fusion.1
  191.0 0.7 constant_dynamic-update-slice_fusion
  191.7 1.5 collective-permute-start.2
  193.2 0.8 constant_dynamic-slice_fusion.traits_ref
  194.0 1.3 collective-permute-done.2
  195.3 0.6 pad_maximum_fusion.1.mean_ref
  195.9 0.0 collective-permute-done.other_ref
  195.9 11.1 %all-gather.3.cloned.1.call-done = bf16[16,64,1024]{2,1,0:T(8,128)(2,1)} async-done(((bf16[2,64,1024]{2,1,0:T(8,128)(2,1)}), bf16[16,64,1024]{2,1,0:T(8,128)(2,1)}) %all-gather.3.cloned.1.call-update) | async-done | bytes 2097168 | tf_op jit(solution)/shard_map/all_gather | solution.py:314
  207.1 9.9 %level_sums.1 = f32[64,128]{1,0:T(8,128)} custom-call(bf16[2048,1024]{1,0:T(8,128)(2,1)} %get-tuple-element.5.own_ref, bf16[2048,1024]{1,0:T(8,128)(2,1)} %collective-permute-done.other_ref, bf16[8,2,64,1024]{3,2,1,0:T(8,128)(2,1)} %bitcast.44, f32[2,1024]{1,0:T(2,128)} %pad_maximum_fusion.1.mean_ref, bf16[2048,64]{1,0:T(8,128)(2,1)} %constant_dynamic-slice_fusion.traits_ref), custom_call_target="tpu_custom_call" | custom-call | tf_op jit(solution)/shard_map/level_sums/pallas_call | solution.py:257
  217.0 40.5 %psum.15 = f32[64,128]{1,0:T(8,128)S(1)} all-reduce(f32[64,128]{1,0:T(8,128)} %level_sums.1), channel_id=1, replica_groups=mesh['samp'=16,'blk'=2] {'samp','blk'}, use_global_device_ids=true, to_apply=%region_1.2 | all-reduce | flops 8192 | bytes 65536 | tf_op jit(solution)/shard_map/psum | solution.py:318
  257.5 0.1 slice.49
  257.6 0.7 copy.16
  258.3 0.1 copy.15
  258.4 0.6 reshape.15
  (6 shorter events, 0.1 us)
Async XLA Ops:
  7.2 123.7 %all-reduce.2.cloned.1.call-start = ((), (), s32[]{:S(2)}) async-start(), calls=%async_computation | async-start | bytes 5308416 | tf_op jit(solution)/shard_map/psum | solution.py:297
  25.7 1.5 copy-start
  27.1 3.1 %copy-start.2 = (s32[5]{0:T(128)S(1)}, s32[5]{0:T(128)}, u32[]{:S(2)}) copy-start(s32[5]{0:T(128)} %param.5) | copy-start | bytes 64
  27.2 179.9 %all-gather.3.cloned.1.call-start = ((), (), s32[]{:S(2)}) async-start(), calls=%async_computation.1 | async-start | bytes 2359296 | tf_op jit(solution)/shard_map/all_gather | solution.py:314
  27.2 168.7 %collective-permute-start = (bf16[2048,1024]{1,0:T(8,128)(2,1)}, bf16[2048,1024]{1,0:T(8,128)(2,1)}, u32[]{:S(2)}, u32[]{:S(2)}) collective-permute-start(bf16[2048,1024]{1,0:T(8,128)(2,1)} %get-tuple-element.6), channel_id=1, source_target_pairs={{0,1},{1,0},{2,3},{3,2},{4,5},{5,4},{6,7},{7,6},{8,9},{9,8},{10,11... | collective-permute-start | bytes 12582920 | tf_op jit(solution)/shard_map/ppermute | solution.py:296
  130.8 1.7 copy-start.1
  180.4 5.0 %collective-permute-start.1 = (bf16[64,1024]{1,0:T(8,128)(2,1)S(1)}, bf16[64,1024]{1,0:T(8,128)(2,1)S(1)}, u32[]{:S(2)}, u32[]{:S(2)}) collective-permute-start(bf16[64,1024]{1,0:T(8,128)(2,1)S(1)} %ridge_solve.1), channel_id=1, source_target_pairs={{0,1},{1,0},{2,3},{3,2},{4,5},{5,4},{6,7},{7,6},{8,9},{9,8},{10,11... | collective-permute-start | bytes 393224 | tf_op jit(solution)/shard_map/ppermute | solution.py:310
  191.7 3.6 %collective-permute-start.2 = (f32[1024]{0:T(1024)S(1)}, f32[1024]{0:T(1024)S(1)}, u32[]{:S(2)}, u32[]{:S(2)}) collective-permute-start(f32[1024]{0:T(1024)S(1)} %broadcast_multiply_fusion), channel_id=1, source_target_pairs={{0,1},{1,0},{2,3},{3,2},{4,5},{5,4},{6,7},{7,6},{8,9},{9,8},{10,11... | collective-permute-start | bytes 12296 | tf_op jit(solution)/shard_map/ppermute | solution.py:309
Sparse Core Ops, SparseCore 0:
  27.3 103.4 all-reduce.1
  186.3 20.6 all-gather.2
